TPU v7x, 256 devices: a whole 4x4x8 slice. The times are simulated.
256 devices in a mesh: attn: 16 (over y_lo, x, core), ffn: 8 (over z), grp: 2 (over y_hi).
Axes of the slice: x: 4, y: 4 (y_hi: 2, y_lo: 2; y = y_hi * 2 + y_lo), z: 8, core: 2. Of those that a mesh axis runs over, the one named last changes fastest.
Arguments:
- query: bfloat16 [2048, 8192], P(('grp', 'attn'), 'ffn'), parts along dimension 0, may hold values from -5 to 5
- key_store_cache: bfloat16 [2048, 192, 1024], P(('grp', 'attn'), None, 'ffn'), parts along dimension 0, may hold values from -5 to 5
- value_store_cache: bfloat16 [2048, 192, 1024], P(('grp', 'attn'), None, 'ffn'), parts along dimension 0, may hold values from -5 to 5
- token_keys: bfloat16 [2048, 1024], P(('grp', 'attn'), 'ffn'), parts along dimension 0, may hold values from -5 to 5
- token_values: bfloat16 [2048, 1024], P(('grp', 'attn'), 'ffn'), parts along dimension 0, may hold values from -5 to 5
- pooled_block_keys: bfloat16 [512, 16, 1024], P(('grp', 'attn'), None, 'ffn'), parts along dimension 0, may hold values from -5 to 5
- pooled_block_values: bfloat16 [512, 16, 1024], P(('grp', 'attn'), None, 'ffn'), parts along dimension 0, may hold values from -6 to 6
- block_dst: int32 [512, 1], P('grp'), parts along dimension 0, may hold values from 0 to 15; in each aligned block of 16 rows (0 to 15, 16 to 31, ...) at most 2 rows name the same one
- block_row: int32 [512], P('grp'), parts along dimension 0, may hold values from 0 to 63
- ctx_len: int32 [2048], P(('grp', 'attn')), parts along dimension 0, may hold values from 1 to 192, as said below
- residual: bfloat16 [2048, 8192], P('grp', 'attn'), parts along dimension 0, may hold values from -15 to 15
- norm_gain: float32 [8192], P('attn'), may hold values from 0.1 to 1.9
- output_weight: bfloat16 [8192, 8192], P('ffn', 'attn'), may hold values from -0.1875 to 0.1875
- w_gate: bfloat16 [8192, 14336], P('attn', 'ffn'), may hold values from -0.0625 to 0.0625
- w_up: bfloat16 [8192, 14336], P('attn', 'ffn'), may hold values from -0.0625 to 0.0625
- w_down: bfloat16 [14336, 8192], P('ffn', 'attn'), may hold values from -0.046875 to 0.046875
Outputs:
- layer_out: bfloat16 [2048, 8192], P(('grp', 'ffn'), 'attn'), parts along dimension 0
There are 2 independent parts, one for each index of `grp`. A program takes and returns all parts, laid end to end along the dimension named above; an argument that names none is the same for every part. Nothing has to cross between parts.
Inputs may be any that keep to these rules, and one draw needn't show every extreme that they name: `block_dst`: of the 16 blocks held by one pool index (aligned blocks of rows), at most 2 name the same attention index. `ctx_len`: every attention index holds a request that uses all 192 cached positions.
All inputs are finite; a program needn't handle non-finite values.
Results may differ from a plain program's by a relative error of at most 0.024.
Values may be sent and summed in bfloat16 or wider, within the bound.
No kernel may reach another device: no remote copies, remote signals or barrier semaphores. Data moves between devices by JAX's collectives and lax.ppermute only.
A program may use at most 128 MiB of HBM per device.

v0:
```python
import jax
import jax.numpy as jnp
from jax import lax
from jax.sharding import PartitionSpec as P

MODEL_WIDTH = 8192
QUERY_HEADS = 64
KEY_VALUE_HEADS = 8
HEAD_SIZE = 128
CAP = 2
epsilon = 1e-05


def body(
    query,
    key_store_cache,
    value_store_cache,
    token_keys,
    token_values,
    pooled_block_keys,
    pooled_block_values,
    block_dst,
    block_row,
    ctx_len,
    residual,
    norm_gain,
    output_weight,
    w_gate,
    w_up,
    w_down,
):
    tok_rows = query.shape[0]
    ctx_size = key_store_cache.shape[1]
    head_width = key_store_cache.shape[2]
    groups = head_width // HEAD_SIZE
    group_rows = QUERY_HEADS // KEY_VALUE_HEADS
    block_len = pooled_block_keys.shape[1]
    local_pool = pooled_block_keys.shape[0]
    attn_size = lax.axis_size("attn")
    my_index = lax.axis_index("attn")
    slot_count = attn_size * CAP
    dst_table = block_dst[:, 0].reshape(attn_size, local_pool)
    row_table = block_row.reshape(attn_size, local_pool)
    positions = jnp.arange(local_pool, dtype=jnp.int32)
    earlier = positions[None, :] < positions[:, None]
    same_dst = dst_table[:, :, None] == dst_table[:, None, :]
    rank_table = jnp.sum((same_dst & earlier[None]).astype(jnp.int32), axis=2)
    own_dst = lax.dynamic_index_in_dim(dst_table, my_index, 0, keepdims=False)
    own_rank = lax.dynamic_index_in_dim(rank_table, my_index, 0, keepdims=False)
    slot_index = own_dst * CAP + own_rank
    picker = (jnp.arange(slot_count, dtype=jnp.int32)[:, None] == slot_index[None, :]).astype(
        jnp.bfloat16
    )
    flat_keys = pooled_block_keys.reshape(local_pool, block_len * head_width)
    flat_values = pooled_block_values.reshape(local_pool, block_len * head_width)
    send_keys = (
        jnp.dot(picker, flat_keys, preferred_element_type=jnp.float32)
        .astype(jnp.bfloat16)
        .reshape(slot_count, block_len, head_width)
    )
    send_values = (
        jnp.dot(picker, flat_values, preferred_element_type=jnp.float32)
        .astype(jnp.bfloat16)
        .reshape(slot_count, block_len, head_width)
    )
    recv_keys, recv_values = (
        lax.all_to_all(send_keys, "attn", split_axis=0, concat_axis=0, tiled=True),
        lax.all_to_all(send_values, "attn", split_axis=0, concat_axis=0, tiled=True),
    )
    cap_slots = jnp.arange(CAP, dtype=jnp.int32)
    hit_mask = (dst_table == my_index)[:, None, :] & (
        rank_table[:, None, :] == cap_slots[None, :, None]
    )
    recv_row = (jnp.sum(jnp.where(hit_mask, row_table[:, None, :] + 1, 0), axis=2) - 1).reshape(
        slot_count
    )
    score_scale = HEAD_SIZE ** (-0.5)
    query_rows = query.reshape(tok_rows, groups, group_rows, HEAD_SIZE)
    stored_keys = key_store_cache.reshape(tok_rows, ctx_size, groups, HEAD_SIZE)
    stored_values = value_store_cache.reshape(tok_rows, ctx_size, groups, HEAD_SIZE)
    score_cache = (
        jnp.einsum("bghd,btgd->bght", query_rows, stored_keys, preferred_element_type=jnp.float32)
        * score_scale
    )
    valid_mask = jnp.arange(ctx_size, dtype=jnp.int32)[None, :] < ctx_len[:, None]
    score_cache = jnp.where(valid_mask[:, None, None, :], score_cache, -jnp.inf)
    resumed_keys = recv_keys.reshape(slot_count * block_len, groups, HEAD_SIZE)
    resumed_values = recv_values.reshape(slot_count * block_len, groups, HEAD_SIZE)
    score_recv = (
        jnp.einsum("bghd,tgd->bght", query_rows, resumed_keys, preferred_element_type=jnp.float32)
        * score_scale
    )
    owner_mask = (
        jnp.repeat(recv_row, block_len)[None, :] == jnp.arange(tok_rows, dtype=jnp.int32)[:, None]
    )
    score_recv = jnp.where(owner_mask[:, None, None, :], score_recv, -jnp.inf)
    current_keys = token_keys.reshape(tok_rows, groups, HEAD_SIZE)
    score_new = (
        jnp.einsum("bghd,bgd->bgh", query_rows, current_keys, preferred_element_type=jnp.float32)
        * score_scale
    )
    row_max = jnp.maximum(
        jnp.maximum(jnp.max(score_cache, axis=-1), jnp.max(score_recv, axis=-1)), score_new
    )
    exp_cache = jnp.exp(score_cache - row_max[..., None])
    exp_recv = jnp.exp(score_recv - row_max[..., None])
    exp_new = jnp.exp(score_new - row_max)
    denominator = jnp.sum(exp_cache, axis=-1) + jnp.sum(exp_recv, axis=-1) + exp_new
    prob_cache = (exp_cache / denominator[..., None]).astype(jnp.bfloat16)
    prob_recv = (exp_recv / denominator[..., None]).astype(jnp.bfloat16)
    prob_new = (exp_new / denominator).astype(jnp.bfloat16)
    weighted = jnp.einsum(
        "bght,btgd->bghd", prob_cache, stored_values, preferred_element_type=jnp.float32
    )
    weighted = weighted + jnp.einsum(
        "bght,tgd->bghd", prob_recv, resumed_values, preferred_element_type=jnp.float32
    )
    current_values = token_values.reshape(tok_rows, groups, HEAD_SIZE).astype(jnp.float32)
    weighted = weighted + prob_new.astype(jnp.float32)[..., None] * current_values[:, :, None, :]
    attended = weighted.reshape(tok_rows, groups * group_rows * HEAD_SIZE).astype(jnp.bfloat16)
    head_part = jnp.dot(
        lax.all_gather(attended, "attn", axis=0, tiled=True),
        output_weight,
        preferred_element_type=jnp.float32,
    )
    ffn_size = lax.axis_size("ffn")
    ffn_index = lax.axis_index("ffn")
    share_rows = head_part.shape[0] // ffn_size
    attn_out = lax.psum(head_part.astype(jnp.bfloat16), "ffn").astype(jnp.float32)
    mixed = residual.astype(jnp.float32) + attn_out
    squares = lax.psum(jnp.sum(mixed * mixed, axis=1), "attn")
    normed = (mixed * lax.rsqrt(squares / MODEL_WIDTH + epsilon)[:, None] * norm_gain).astype(
        jnp.bfloat16
    )
    kept_rows = lax.dynamic_slice_in_dim(mixed, ffn_index * share_rows, share_rows, 0)
    hidden_width = w_gate.shape[1]
    gate_up = lax.psum_scatter(
        jnp.concatenate(
            [
                jnp.dot(normed, w_gate, preferred_element_type=jnp.float32),
                jnp.dot(normed, w_up, preferred_element_type=jnp.float32),
            ],
            axis=1,
        ).astype(jnp.bfloat16),
        "attn",
        scatter_dimension=0,
        tiled=True,
    ).astype(jnp.float32)
    activated = (jax.nn.silu(gate_up[:, :hidden_width]) * gate_up[:, hidden_width:]).astype(
        jnp.bfloat16
    )
    down_part = jnp.dot(
        lax.all_gather(activated, "attn", axis=0, tiled=True),
        w_down,
        preferred_element_type=jnp.float32,
    )
    ffn_share = lax.psum_scatter(
        down_part.astype(jnp.bfloat16), "ffn", scatter_dimension=0, tiled=True
    ).astype(jnp.float32)
    return (kept_rows + ffn_share).astype(jnp.bfloat16)


def solution(mesh):
    placed = (
        P(("grp", "attn"), "ffn"),
        P(("grp", "attn"), None, "ffn"),
        P(("grp", "attn"), None, "ffn"),
        P(("grp", "attn"), "ffn"),
        P(("grp", "attn"), "ffn"),
        P(("grp", "attn"), None, "ffn"),
        P(("grp", "attn"), None, "ffn"),
        P("grp", None),
        P("grp"),
        P(("grp", "attn")),
        P("grp", "attn"),
        P("attn"),
        P("ffn", "attn"),
        P("attn", "ffn"),
        P("attn", "ffn"),
        P("ffn", "attn"),
    )
    return jax.shard_map(
        body, mesh=mesh, in_specs=placed, out_specs=P(("grp", "ffn"), "attn"), check_vma=False
    )
```

profile of v0, /device:TPU:2, one launch (start us, length us, event | category | flops | bytes accessed | tf_op | source)
XLA Modules:
  0.0 378.0 jit_solution(17119664770401599803)
XLA Ops:
  6.5 0.5 broadcast.96
  7.1 1.6 reduce.9
  8.7 0.1 reshape_squeeze.3
  8.7 0.4 convert_reduce_fusion
  9.2 1.0 fusion.6
  10.2 0.7 copy.58
  10.9 5.9 %all-to-all-start = ((bf16[32,16,128]{2,1,0:T(8,128)(2,1)}), bf16[32,16,128]{2,1,0:T(8,128)(2,1)S(1)}, u32[]{:S(2)}, u32[]{:S(2)}) async-start(bf16[32,16,128]{2,1,0:T(8,128)(2,1)} %bitcast.24), calls=%async_computation | async-start | bytes 262144 | tf_op jit(solution)/shard_map/all_to_all | solution.py:67
  16.8 0.7 broadcast_add_fusion.1
  17.4 0.1 add.69
  17.5 0.1 select_reduce_fusion
  17.6 0.1 copy.43
  17.7 0.1 sub.28
  17.8 0.1 broadcast_in_dim.42
  17.9 0.7 eq.78
  18.6 0.7 iota_compare_fusion.1
  19.3 1.3 convert_element_type.71
  20.6 1.0 fusion.7
  21.6 0.7 copy.60
  22.3 0.9 copy.56
  23.2 0.9 fusion.21
  24.2 0.7 copy.52
  24.8 3.2 fusion.30
  28.0 0.8 copy.45
  28.8 0.7 iota_compare_fusion
  29.5 5.7 %all-to-all-start.1 = ((bf16[32,16,128]{2,1,0:T(8,128)(2,1)}), bf16[32,16,128]{2,1,0:T(8,128)(2,1)}, u32[]{:S(2)}, u32[]{:S(2)}) async-start(bf16[32,16,128]{2,1,0:T(8,128)(2,1)} %bitcast.28), calls=%async_computation.1 | async-start | bytes 262144 | tf_op jit(solution)/shard_map/all_to_all | solution.py:68
  35.3 0.0 all-gather.3.cloned.1.call-start
  35.3 1.3 fusion.31
  36.6 0.7 maximum_maximum_fusion
  37.3 0.1 copy.46
  37.4 1.5 fusion.8
  38.9 1.3 fusion.11
  40.2 0.1 copy.47
  40.3 0.1 copy.48
  40.4 3.1 convolution_bitcast_fusion.1
  43.5 1.1 fusion.10
  44.6 0.1 copy.50
  44.7 1.5 fusion.5
  46.2 0.7 copy.81
  46.9 0.0 all-gather.3.cloned.1.call-update
  46.9 0.0 all-reduce.2.cloned.1.call-start
  47.0 38.8 %all-gather.3.cloned.1.call-done = bf16[1024,1024]{1,0:T(8,128)(2,1)} async-done(((bf16[64,1024]{1,0:T(8,128)(2,1)}), bf16[1024,1024]{1,0:T(8,128)(2,1)}) %all-gather.3.cloned.1.call-update) | async-done | bytes 2097168 | tf_op jit(solution)/shard_map/all_gather | solution.py:122
  85.8 4.1 %convolution_convert_fusion.4 = bf16[1024,512]{1,0:T(8,128)(2,1)} fusion(bf16[1024,1024]{1,0:T(8,128)(2,1)} %all-gather.3.cloned.1.call-done, bf16[1024,512]{1,0:T(8,128)(2,1)} %param.28), kind=kOutput, calls=%fused_computation.8 | convolution fusion | flops 1074266112 | bytes 4194304 | tf_op jit(solution)/shard_map/dot_general | solution.py:121
  89.9 0.0 all-reduce.2.cloned.1.call-update
  89.9 0.0 reduce-scatter.3.cloned.1.call-start
  90.0 76.5 %all-reduce.2.cloned.1.call-done = bf16[1024,512]{1,0:T(8,128)(2,1)} async-done(((bf16[1024,512]{1,0:T(8,128)(2,1)}), bf16[1024,512]{1,0:T(8,128)(2,1)}) %all-reduce.2.cloned.1.call-update) | async-done | bytes 1048592 | tf_op jit(solution)/shard_map/psum | solution.py:129
  166.5 3.2 convert_add_fusion
  169.7 23.6 %psum.15 = f32[1024]{0:T(1024)S(1)} all-reduce(f32[1024]{0:T(1024)S(1)} %get-tuple-element.8), channel_id=1, replica_groups=mesh['attn'=16,'ffn'=8,'grp'=2] {'attn'}, use_global_device_ids=true, to_apply=%region_8.9 | all-reduce | flops 1024 | bytes 8192 | tf_op jit(solution)/shard_map/psum | solution.py:131
  193.3 0.0 copy-start.2
  193.4 0.0 copy-start.7
  193.4 6.4 %convolution_convert_fusion = bf16[1024,1792]{1,0:T(8,128)(2,1)} fusion(bf16[512,1792]{1,0:T(8,128)(2,1)} %param.30, f32[512]{0:T(512)S(1)} %copy-done.8, f32[1024]{0:T(1024)S(1)} %add_rsqrt_fusion, bf16[1024,512]{1,0:T(8,128)(2,1)} %all-reduce.2.cloned.1.call-done, bf16[1024,512]{1,0:T(8,128)(2,1)} %param.26), kind=kOutput, calls=%fused_computation.1 | convolution fusion | flops 1884028928 | bytes 7608320 | tf_op jit(solution)/shard_map/dot_general | solution.py:141
  199.8 4.2 %convolution_convert_fusion.1 = bf16[1024,1792]{1,0:T(8,128)(2,1)} fusion(bf16[512,1792]{1,0:T(8,128)(2,1)S(1)} %copy-done.7, f32[512]{0:T(512)S(1)} %copy-done.8, f32[1024]{0:T(1024)S(1)} %add_rsqrt_fusion, bf16[1024,512]{1,0:T(8,128)(2,1)S(1)} %copy-done.3, bf16[1024,512]{1,0:T(8,128)(2,1)S(1)} %copy-done.2), kind=kOutput, calls=%fused_computation.2 | convolution fusion | flops 1884028928 | bytes 7608320 | tf_op jit(solution)/shard_map/dot_general | solution.py:140
  204.0 6.6 %pad_maximum_fusion = bf16[1024,3584]{1,0:T(8,128)(2,1)} fusion(bf16[1024,1792]{1,0:T(8,128)(2,1)} %convolution_convert_fusion, bf16[1024,1792]{1,0:T(8,128)(2,1)} %convolution_convert_fusion.1), kind=kLoop, calls=%fused_computation | loop fusion | flops 14680064 | bytes 14680064 | tf_op jit(solution)/shard_map/concatenate | solution.py:138
  210.6 0.0 reduce-scatter.3.cloned.1.call-update
  210.6 0.0 all-gather.5.cloned.1.call-start
  210.7 70.3 %reduce-scatter.3.cloned.1.call-done = bf16[64,3584]{1,0:T(8,128)(2,1)} async-done(((bf16[1024,3584]{1,0:T(8,128)(2,1)}), bf16[64,3584]{1,0:T(8,128)(2,1)}) %reduce-scatter.3.cloned.1.call-update) | async-done | bytes 458768 | tf_op jit(solution)/shard_map/reduce_scatter | solution.py:137
  281.0 1.1 convert_element_type.77
  282.1 0.8 fusion.12
  282.9 0.0 all-gather.5.cloned.1.call-update
  282.9 0.0 reduce-scatter.5.cloned.1.call-start
  283.0 42.0 %all-gather.5.cloned.1.call-done = bf16[1024,1792]{1,0:T(8,128)(2,1)} async-done(((bf16[64,1792]{1,0:T(8,128)(2,1)}), bf16[1024,1792]{1,0:T(8,128)(2,1)}) %all-gather.5.cloned.1.call-update) | async-done | bytes 3670032 | tf_op jit(solution)/shard_map/all_gather | solution.py:153
  325.0 5.6 %convolution_convert_fusion.5 = bf16[1024,512]{1,0:T(8,128)(2,1)} fusion(bf16[1024,1792]{1,0:T(8,128)(2,1)} %all-gather.5.cloned.1.call-done, bf16[1792,512]{1,0:T(8,128)(2,1)} %param.31), kind=kOutput, calls=%fused_computation.9 | convolution fusion | flops 1879572480 | bytes 6553600 | tf_op jit(solution)/shard_map/dot_general | solution.py:152
  330.6 0.0 reduce-scatter.5.cloned.1.call-update
  330.6 39.2 %reduce-scatter.5.cloned.1.call-done = bf16[128,512]{1,0:T(8,128)(2,1)} async-done(((bf16[1024,512]{1,0:T(8,128)(2,1)}), bf16[128,512]{1,0:T(8,128)(2,1)}) %reduce-scatter.5.cloned.1.call-update) | async-done | bytes 131088 | tf_op jit(solution)/shard_map/reduce_scatter | solution.py:157
  369.8 1.7 add_convert_fusion
  (24 shorter events, 0.1 us)
Async XLA Ops:
  6.5 18.3 %copy-start = (bf16[64,192,128]{2,1,0:T(8,128)(2,1)S(1)}, bf16[64,192,128]{2,1,0:T(8,128)(2,1)}, u32[]{:S(2)}) copy-start(bf16[64,192,128]{2,1,0:T(8,128)(2,1)} %param.17) | copy-start | bytes 9437188
  10.9 18.6 %all-to-all-start = ((bf16[32,16,128]{2,1,0:T(8,128)(2,1)}), bf16[32,16,128]{2,1,0:T(8,128)(2,1)S(1)}, u32[]{:S(2)}, u32[]{:S(2)}) async-start(bf16[32,16,128]{2,1,0:T(8,128)(2,1)} %bitcast.24), calls=%async_computation | async-start | bytes 262144 | tf_op jit(solution)/shard_map/all_to_all | solution.py:67
  24.8 10.5 %copy-start.4 = (bf16[64,1024]{1,0:T(8,128)(2,1)S(1)}, bf16[64,1024]{1,0:T(8,128)(2,1)}, u32[]{:S(2)}) copy-start(bf16[64,1024]{1,0:T(8,128)(2,1)} %param.16) | copy-start | bytes 393220
  28.0 12.3 %copy-start.5 = (f32[64,1,8]{0,2,1:T(8,128)S(1)}, f32[64,1,8]{0,2,1:T(8,128)}, u32[]{:S(2)}) copy-start(f32[64,1,8]{0,2,1:T(8,128)} %copy.52) | copy-start | bytes 6148
  29.5 15.1 %all-to-all-start.1 = ((bf16[32,16,128]{2,1,0:T(8,128)(2,1)}), bf16[32,16,128]{2,1,0:T(8,128)(2,1)}, u32[]{:S(2)}, u32[]{:S(2)}) async-start(bf16[32,16,128]{2,1,0:T(8,128)(2,1)} %bitcast.28), calls=%async_computation.1 | async-start | bytes 262144 | tf_op jit(solution)/shard_map/all_to_all | solution.py:68
  35.3 50.5 %all-gather.3.cloned.1.call-start = ((), (), s32[]{:S(2)}) async-start(), calls=%async_computation.4 | async-start | bytes 2228224 | tf_op jit(solution)/shard_map/all_gather | solution.py:122
  40.4 3.1 copy-start.1
  40.4 4.3 %copy-start.6 = (f32[64,128]{1,0:T(8,128)S(1)}, f32[64,128]{1,0:T(8,128)}, u32[]{:S(2)}) copy-start(f32[64,128]{1,0:T(8,128)} %convert_element_type.71) | copy-start | bytes 98308
  46.9 119.6 %all-reduce.2.cloned.1.call-start = ((), (), s32[]{:S(2)}) async-start(), calls=%async_computation.5 | async-start | bytes 2097152 | tf_op jit(solution)/shard_map/psum | solution.py:129
  89.9 103.4 %copy-start.8 = (f32[512]{0:T(512)S(1)}, f32[512]{0:T(512)}, u32[]{:S(2)}) copy-start(f32[512]{0:T(512)} %param.27) | copy-start | bytes 6148
  89.9 191.1 %reduce-scatter.3.cloned.1.call-start = ((), (), s32[]{:S(2)}) async-start(), calls=%async_computation.6 | async-start | bytes 7798784 | tf_op jit(solution)/shard_map/reduce_scatter | solution.py:137
  193.3 6.4 %copy-start.2 = (bf16[1024,512]{1,0:T(8,128)(2,1)S(1)}, bf16[1024,512]{1,0:T(8,128)(2,1)}, u32[]{:S(2)}) copy-start(bf16[1024,512]{1,0:T(8,128)(2,1)} %param.26) | copy-start | bytes 3145732
  193.4 6.4 %copy-start.3 = (bf16[1024,512]{1,0:T(8,128)(2,1)S(1)}, bf16[1024,512]{1,0:T(8,128)(2,1)}, u32[]{:S(2)}) copy-start(bf16[1024,512]{1,0:T(8,128)(2,1)} %all-reduce.2.cloned.1.call-done) | copy-start | bytes 3145732
  193.4 6.4 %copy-start.7 = (bf16[512,1792]{1,0:T(8,128)(2,1)S(1)}, bf16[512,1792]{1,0:T(8,128)(2,1)}, u32[]{:S(2)}) copy-start(bf16[512,1792]{1,0:T(8,128)(2,1)} %param.29) | copy-start | bytes 5505028
  210.6 114.3 %all-gather.5.cloned.1.call-start = ((), (), s32[]{:S(2)}) async-start(), calls=%async_computation.7 | async-start | bytes 3899392 | tf_op jit(solution)/shard_map/all_gather | solution.py:153
  282.9 86.8 %reduce-scatter.5.cloned.1.call-start = ((), (), s32[]{:S(2)}) async-start(), calls=%async_computation.8 | async-start | bytes 1179648 | tf_op jit(solution)/shard_map/reduce_scatter | solution.py:157
Sparse Core Ops, SparseCore 0:
  47.0 38.7 all-gather.2
  90.0 76.4 all-reduce.1
  210.8 70.1 reduce-scatter.2
  283.0 41.8 all-gather.4
  330.7 38.9 reduce-scatter.4
where the time goes:
time: 379 us; the launch traced here: 378 us
  waiting for transfers between devices  267 us (70%)
  matrix products  32.3 us (9%)
  other arithmetic  23.7 us (6%)
  blocking collectives  23.6 us (6%)
  between operations  13.3 us (4%)
  starting transfers between devices  11.8 us (3%)
  local copies, waits for them, and re-layouts  6.4 us (2%)
    psum x1, waiting for transfers between devices, body(): lax.psum(head_part.astype(jnp.bfloat16), 'ffn').astype(jnp.float32)  76.5 us
    reduce_scatter x1, waiting for transfers between devices, body(): lax.psum_scatter(jnp.concatenate([jnp.dot(normed, w_gate, preferred_eleme...  70.3 us
    all_gather x1, waiting for transfers between devices, body(): lax.all_gather(activated, 'attn', axis=0, tiled=True)  42 us
    reduce_scatter x1, waiting for transfers between devices, body(): lax.psum_scatter(down_part.astype(jnp.bfloat16), 'ffn', scatter_dimension...  39.2 us
    all_gather x1, waiting for transfers between devices, body(): lax.all_gather(attended, 'attn', axis=0, tiled=True)  38.8 us
    psum x1, blocking collectives, body(): squares = lax.psum(jnp.sum(mixed * mixed, axis=1), 'attn')  23.6 us
  transfers between devices with their start and end apart: 7, of which 5 were waited for; matrix products, arithmetic and copies ran while one was open for 6% of the time, Pallas kernels for 0%

commit v1 on v0

--- a/solution.py
+++ b/solution.py
@@ -126,7 +126,9 @@
     ffn_size = lax.axis_size("ffn")
     ffn_index = lax.axis_index("ffn")
     share_rows = head_part.shape[0] // ffn_size
-    attn_out = lax.psum(head_part.astype(jnp.bfloat16), "ffn").astype(jnp.float32)
+    attn_out = jnp.sum(lax.all_gather(head_part.astype(jnp.bfloat16), "ffn"), axis=0).astype(
+        jnp.float32
+    )
     mixed = residual.astype(jnp.float32) + attn_out
     squares = lax.psum(jnp.sum(mixed * mixed, axis=1), "attn")
     normed = (mixed * lax.rsqrt(squares / MODEL_WIDTH + epsilon)[:, None] * norm_gain).astype(

time: 379 us -> 406 us (1.071)
  waiting for transfers between devices: 267 us -> 286 us
  other arithmetic: 23.7 us -> 29.5 us
    all_gather x0 -> x1, waiting for transfers between devices: none -> 94.8 us  [body(): lax.all_gather(head_part.astype(jnp.bfloat16), 'ffn')]
    psum x1 -> x0, waiting for transfers between devices: 76.5 us -> none  [body(): lax.psum(head_part.astype(jnp.bfloat16), 'ffn').astype(jnp.float32)]
    reduce_sum x0 -> x1, other arithmetic: none -> 5.86 us  [body(): jnp.sum(lax.all_gather(head_part.astype(jnp.bfloat16), 'ffn'), axis=0)]
  transfers between devices with their start and end apart: 7 -> 7, of which waited for: 5 -> 5; matrix products, arithmetic and copies ran while one was open for 6% -> 5% of each run, Pallas kernels for 0% -> 0%
where the time goes in v1:
time: 406 us
  waiting for transfers between devices  286 us (70%)
  matrix products  32.4 us (8%)
  other arithmetic  29.5 us (7%)
  blocking collectives  26.5 us (7%)
  between operations  13.3 us (3%)
  starting transfers between devices  11.8 us (3%)
  local copies, waits for them, and re-layouts  6.39 us (2%)
    all_gather x1, waiting for transfers between devices, body(): lax.all_gather(head_part.astype(jnp.bfloat16), 'ffn')  94.8 us
    reduce_scatter x1, waiting for transfers between devices, body(): lax.psum_scatter(jnp.concatenate([jnp.dot(normed, w_gate, preferred_eleme...  70.6 us
    all_gather x1, waiting for transfers between devices, body(): lax.all_gather(activated, 'attn', axis=0, tiled=True)  42.1 us
    reduce_scatter x1, waiting for transfers between devices, body(): lax.psum_scatter(down_part.astype(jnp.bfloat16), 'ffn', scatter_dimension...  39.2 us
    all_gather x1, waiting for transfers between devices, body(): lax.all_gather(attended, 'attn', axis=0, tiled=True)  38.8 us
    psum x1, blocking collectives, body(): squares = lax.psum(jnp.sum(mixed * mixed, axis=1), 'attn')  26.5 us
  transfers between devices with their start and end apart: 7, of which 5 were waited for; matrix products, arithmetic and copies ran while one was open for 5% of the time, Pallas kernels for 0%

profile of v1, /device:TPU:2, one launch (start us, length us, event | category | flops | bytes accessed | tf_op | source)
XLA Modules:
  0.0 405.6 jit_solution(8091418922527118570)
XLA Ops:
  6.5 0.5 broadcast.96
  7.1 1.6 reduce.10
  8.7 0.1 reshape_squeeze.3
  8.7 0.4 convert_reduce_fusion
  9.2 1.0 fusion.6
  10.2 0.7 copy.58
  10.9 5.9 %all-to-all-start = ((bf16[32,16,128]{2,1,0:T(8,128)(2,1)}), bf16[32,16,128]{2,1,0:T(8,128)(2,1)S(1)}, u32[]{:S(2)}, u32[]{:S(2)}) async-start(bf16[32,16,128]{2,1,0:T(8,128)(2,1)} %bitcast.25), calls=%async_computation | async-start | bytes 262144 | tf_op jit(solution)/shard_map/all_to_all | solution.py:67
  16.8 0.7 broadcast_add_fusion.1
  17.4 0.1 add.67
  17.5 0.1 select_reduce_fusion
  17.6 0.1 copy.43
  17.7 0.1 sub.28
  17.8 0.1 broadcast_in_dim.42
  17.9 0.7 eq.78
  18.6 0.7 iota_compare_fusion.1
  19.3 1.3 convert_element_type.73
  20.6 1.0 fusion.7
  21.6 0.7 copy.60
  22.3 0.9 copy.56
  23.2 0.9 fusion.21
  24.2 0.7 copy.52
  24.8 3.2 fusion.30
  28.0 0.8 copy.45
  28.8 0.7 iota_compare_fusion
  29.5 5.7 %all-to-all-start.1 = ((bf16[32,16,128]{2,1,0:T(8,128)(2,1)}), bf16[32,16,128]{2,1,0:T(8,128)(2,1)}, u32[]{:S(2)}, u32[]{:S(2)}) async-start(bf16[32,16,128]{2,1,0:T(8,128)(2,1)} %bitcast.29), calls=%async_computation.1 | async-start | bytes 262144 | tf_op jit(solution)/shard_map/all_to_all | solution.py:68
  35.3 0.0 all-gather.5.cloned.1.call-start
  35.3 1.3 fusion.31
  36.6 0.7 maximum_maximum_fusion
  37.3 0.1 copy.46
  37.4 1.5 fusion.8
  38.9 1.3 fusion.11
  40.2 0.1 copy.47
  40.3 0.1 copy.48
  40.4 3.1 convolution_bitcast_fusion.1
  43.5 1.1 fusion.10
  44.6 0.1 copy.50
  44.7 1.5 fusion.5
  46.2 0.7 copy.81
  46.9 0.0 all-gather.5.cloned.1.call-update
  46.9 0.0 all-gather.9.cloned.1.call-start
  47.0 38.8 %all-gather.5.cloned.1.call-done = bf16[1024,1024]{1,0:T(8,128)(2,1)} async-done(((bf16[64,1024]{1,0:T(8,128)(2,1)}), bf16[1024,1024]{1,0:T(8,128)(2,1)}) %all-gather.5.cloned.1.call-update) | async-done | bytes 2097168 | tf_op jit(solution)/shard_map/all_gather | solution.py:122
  85.8 4.2 %convolution_convert_fusion.4 = bf16[1024,512]{1,0:T(8,128)(2,1)} fusion(bf16[1024,1024]{1,0:T(8,128)(2,1)} %all-gather.5.cloned.1.call-done, bf16[1024,512]{1,0:T(8,128)(2,1)} %param.28), kind=kOutput, calls=%fused_computation.8 | convolution fusion | flops 1074266112 | bytes 4194304 | tf_op jit(solution)/shard_map/dot_general | solution.py:121
  90.0 0.0 all-gather.9.cloned.1.call-update
  90.0 0.0 reduce-scatter.3.cloned.1.call-start
  90.0 94.8 %all-gather.9.cloned.1.call-done = bf16[8192,512]{1,0:T(8,128)(2,1)} async-done(((bf16[1024,512]{1,0:T(8,128)(2,1)}), bf16[8192,512]{1,0:T(8,128)(2,1)}) %all-gather.9.cloned.1.call-update) | async-done | bytes 8388624 | tf_op jit(solution)/shard_map/all_gather | solution.py:129
  184.8 5.9 %reduce_sum.61 = bf16[1024,512]{1,0:T(8,128)(2,1)} reduce(bf16[8,1024,512]{2,1,0:T(8,128)(2,1)} %bitcast.85, bf16[]{:T(256)} %constant.41.clone.1), dimensions={0}, to_apply=%region_6.7 | reduce | flops 3670016 | bytes 9437186 | tf_op jit(solution)/shard_map/reduce_sum | solution.py:129
  190.7 3.2 convert_add_fusion
  193.9 26.5 %psum.7 = f32[1024]{0:T(1024)S(1)} all-reduce(f32[1024]{0:T(1024)S(1)} %get-tuple-element.8), channel_id=1, replica_groups=mesh['attn'=16,'ffn'=8,'grp'=2] {'attn'}, use_global_device_ids=true, to_apply=%region_8.9 | all-reduce | flops 1024 | bytes 8192 | tf_op jit(solution)/shard_map/psum | solution.py:133
  220.4 0.0 copy-start.3
  220.5 6.4 %convolution_convert_fusion = bf16[1024,1792]{1,0:T(8,128)(2,1)} fusion(bf16[512,1792]{1,0:T(8,128)(2,1)} %param.30, f32[512]{0:T(512)S(1)} %copy-done.8, f32[1024]{0:T(1024)S(1)} %add_rsqrt_fusion, bf16[1024,512]{1,0:T(8,128)(2,1)} %reduce_sum.61, bf16[1024,512]{1,0:T(8,128)(2,1)} %param.26), kind=kOutput, calls=%fused_computation.1 | convolution fusion | flops 1884028928 | bytes 7608320 | tf_op jit(solution)/shard_map/dot_general | solution.py:143
  226.9 4.2 %convolution_convert_fusion.1 = bf16[1024,1792]{1,0:T(8,128)(2,1)} fusion(bf16[512,1792]{1,0:T(8,128)(2,1)S(1)} %copy-done.7, f32[512]{0:T(512)S(1)} %copy-done.8, f32[1024]{0:T(1024)S(1)} %add_rsqrt_fusion, bf16[1024,512]{1,0:T(8,128)(2,1)S(1)} %copy-done.2, bf16[1024,512]{1,0:T(8,128)(2,1)S(1)} %copy-done.3), kind=kOutput, calls=%fused_computation.2 | convolution fusion | flops 1884028928 | bytes 7608320 | tf_op jit(solution)/shard_map/dot_general | solution.py:142
  231.1 6.6 %pad_maximum_fusion = bf16[1024,3584]{1,0:T(8,128)(2,1)} fusion(bf16[1024,1792]{1,0:T(8,128)(2,1)} %convolution_convert_fusion, bf16[1024,1792]{1,0:T(8,128)(2,1)} %convolution_convert_fusion.1), kind=kLoop, calls=%fused_computation | loop fusion | flops 14680064 | bytes 14680064 | tf_op jit(solution)/shard_map/concatenate | solution.py:140
  237.7 0.0 reduce-scatter.3.cloned.1.call-update
  237.7 0.0 all-gather.7.cloned.1.call-start
  237.8 70.6 %reduce-scatter.3.cloned.1.call-done = bf16[64,3584]{1,0:T(8,128)(2,1)} async-done(((bf16[1024,3584]{1,0:T(8,128)(2,1)}), bf16[64,3584]{1,0:T(8,128)(2,1)}) %reduce-scatter.3.cloned.1.call-update) | async-done | bytes 458768 | tf_op jit(solution)/shard_map/reduce_scatter | solution.py:139
  308.4 1.1 convert_element_type.79
  309.5 0.8 fusion.12
  310.3 0.0 all-gather.7.cloned.1.call-update
  310.3 0.0 reduce-scatter.5.cloned.1.call-start
  310.4 42.1 %all-gather.7.cloned.1.call-done = bf16[1024,1792]{1,0:T(8,128)(2,1)} async-done(((bf16[64,1792]{1,0:T(8,128)(2,1)}), bf16[1024,1792]{1,0:T(8,128)(2,1)}) %all-gather.7.cloned.1.call-update) | async-done | bytes 3670032 | tf_op jit(solution)/shard_map/all_gather | solution.py:155
  352.5 5.6 %convolution_convert_fusion.5 = bf16[1024,512]{1,0:T(8,128)(2,1)} fusion(bf16[1024,1792]{1,0:T(8,128)(2,1)} %all-gather.7.cloned.1.call-done, bf16[1792,512]{1,0:T(8,128)(2,1)} %param.31), kind=kOutput, calls=%fused_computation.9 | convolution fusion | flops 1879572480 | bytes 6553600 | tf_op jit(solution)/shard_map/dot_general | solution.py:154
  358.1 0.0 reduce-scatter.5.cloned.1.call-update
  358.2 39.2 %reduce-scatter.5.cloned.1.call-done = bf16[128,512]{1,0:T(8,128)(2,1)} async-done(((bf16[1024,512]{1,0:T(8,128)(2,1)}), bf16[128,512]{1,0:T(8,128)(2,1)}) %reduce-scatter.5.cloned.1.call-update) | async-done | bytes 131088 | tf_op jit(solution)/shard_map/reduce_scatter | solution.py:159
  397.4 1.7 add_convert_fusion
  (25 shorter events, 0.1 us)
Async XLA Ops:
  6.5 18.3 %copy-start = (bf16[64,192,128]{2,1,0:T(8,128)(2,1)S(1)}, bf16[64,192,128]{2,1,0:T(8,128)(2,1)}, u32[]{:S(2)}) copy-start(bf16[64,192,128]{2,1,0:T(8,128)(2,1)} %param.17) | copy-start | bytes 9437188
  10.9 18.6 %all-to-all-start = ((bf16[32,16,128]{2,1,0:T(8,128)(2,1)}), bf16[32,16,128]{2,1,0:T(8,128)(2,1)S(1)}, u32[]{:S(2)}, u32[]{:S(2)}) async-start(bf16[32,16,128]{2,1,0:T(8,128)(2,1)} %bitcast.25), calls=%async_computation | async-start | bytes 262144 | tf_op jit(solution)/shard_map/all_to_all | solution.py:67
  24.8 10.5 %copy-start.4 = (bf16[64,1024]{1,0:T(8,128)(2,1)S(1)}, bf16[64,1024]{1,0:T(8,128)(2,1)}, u32[]{:S(2)}) copy-start(bf16[64,1024]{1,0:T(8,128)(2,1)} %param.16) | copy-start | bytes 393220
  28.0 12.3 %copy-start.5 = (f32[64,1,8]{0,2,1:T(8,128)S(1)}, f32[64,1,8]{0,2,1:T(8,128)}, u32[]{:S(2)}) copy-start(f32[64,1,8]{0,2,1:T(8,128)} %copy.52) | copy-start | bytes 6148
  29.5 15.1 %all-to-all-start.1 = ((bf16[32,16,128]{2,1,0:T(8,128)(2,1)}), bf16[32,16,128]{2,1,0:T(8,128)(2,1)}, u32[]{:S(2)}, u32[]{:S(2)}) async-start(bf16[32,16,128]{2,1,0:T(8,128)(2,1)} %bitcast.29), calls=%async_computation.1 | async-start | bytes 262144 | tf_op jit(solution)/shard_map/all_to_all | solution.py:68
  35.3 50.5 %all-gather.5.cloned.1.call-start = ((), (), s32[]{:S(2)}) async-start(), calls=%async_computation.4 | async-start | bytes 2228224 | tf_op jit(solution)/shard_map/all_gather | solution.py:122
  40.4 3.1 copy-start.1
  40.4 4.3 %copy-start.6 = (f32[64,128]{1,0:T(8,128)S(1)}, f32[64,128]{1,0:T(8,128)}, u32[]{:S(2)}) copy-start(f32[64,128]{1,0:T(8,128)} %convert_element_type.73) | copy-start | bytes 98308
  46.9 137.9 %all-gather.9.cloned.1.call-start = ((), (), s32[]{:S(2)}) async-start(), calls=%async_computation.8 | async-start | bytes 9437184 | tf_op jit(solution)/shard_map/all_gather | solution.py:129
  90.0 218.4 %reduce-scatter.3.cloned.1.call-start = ((), (), s32[]{:S(2)}) async-start(), calls=%async_computation.5 | async-start | bytes 7798784 | tf_op jit(solution)/shard_map/reduce_scatter | solution.py:139
  190.7 29.7 %copy-start.8 = (f32[512]{0:T(512)S(1)}, f32[512]{0:T(512)}, u32[]{:S(2)}) copy-start(f32[512]{0:T(512)} %param.27) | copy-start | bytes 6148
  220.4 6.4 %copy-start.2 = (bf16[1024,512]{1,0:T(8,128)(2,1)S(1)}, bf16[1024,512]{1,0:T(8,128)(2,1)}, u32[]{:S(2)}) copy-start(bf16[1024,512]{1,0:T(8,128)(2,1)} %reduce_sum.61) | copy-start | bytes 3145732
  220.4 6.4 %copy-start.3 = (bf16[1024,512]{1,0:T(8,128)(2,1)S(1)}, bf16[1024,512]{1,0:T(8,128)(2,1)}, u32[]{:S(2)}) copy-start(bf16[1024,512]{1,0:T(8,128)(2,1)} %param.26) | copy-start | bytes 3145732
  220.5 6.4 %copy-start.7 = (bf16[512,1792]{1,0:T(8,128)(2,1)S(1)}, bf16[512,1792]{1,0:T(8,128)(2,1)}, u32[]{:S(2)}) copy-start(bf16[512,1792]{1,0:T(8,128)(2,1)} %param.29) | copy-start | bytes 5505028
  237.7 114.8 %all-gather.7.cloned.1.call-start = ((), (), s32[]{:S(2)}) async-start(), calls=%async_computation.6 | async-start | bytes 3899392 | tf_op jit(solution)/shard_map/all_gather | solution.py:155
  310.3 87.0 %reduce-scatter.5.cloned.1.call-start = ((), (), s32[]{:S(2)}) async-start(), calls=%async_computation.7 | async-start | bytes 1179648 | tf_op jit(solution)/shard_map/reduce_scatter | solution.py:159
Sparse Core Ops, SparseCore 0:
  47.0 38.7 all-gather.4
  90.1 94.6 all-gather.8
  237.8 70.5 reduce-scatter.2
  310.5 42.0 all-gather.6
  358.3 39.0 reduce-scatter.4
